TPU v7x, 32 devices: a whole 2x2x4 slice. The times are simulated.
32 devices in a mesh: rep: 8 (over y, x, core), exp: 4 (over z).
Axes of the slice: x: 2, y: 2, z: 4, core: 2. Of those that a mesh axis runs over, the one named last changes fastest.
Arguments:
- tokens: bfloat16 [64, 197, 768], P(('rep', 'exp')), may hold values from -6 to 6
- routes: int32 [64, 197, 2], P(('rep', 'exp')), may hold values from 0 to 3, all different within a row; in each aligned block of 394 rows (0 to 393, 394 to 787, ..., all dimensions but the last counted through in order) at most 264 rows name the same one
- cotangent: bfloat16 [64, 197, 768], P(('rep', 'exp')), may hold values from -6 to 6
- attn_gain: bfloat16 [768], P('exp'), may hold values from 0.099609375 to 1.8984375
- attn_shift: bfloat16 [768], P('exp'), may hold values from -3 to 3
- qkv_weight: bfloat16 [768, 2304], P('exp'), may hold values from -0.21875 to 0.21875
- query_bias: bfloat16 [768], P('exp'), may hold values from -3 to 3
- value_bias: bfloat16 [768], P('exp'), may hold values from -3 to 3
- proj_weight: bfloat16 [768, 768], P('exp'), may hold values from -0.875 to 0.875
- proj_bias: bfloat16 [768], P('exp'), may hold values from -3 to 3
- moe_gain: bfloat16 [768], P('exp'), may hold values from 0.099609375 to 1.8984375
- moe_shift: bfloat16 [768], P('exp'), may hold values from -3 to 3
- router_weight: bfloat16 [768, 4], P('exp'), may hold values from -0.21875 to 0.21875
- expert_in: bfloat16 [4, 768, 3072], P('exp'), may hold values from -0.21875 to 0.21875
- expert_in_bias: bfloat16 [4, 3072], P('exp'), may hold values from -3 to 3
- expert_out: bfloat16 [4, 3072, 768], P('exp'), may hold values from -0.4375 to 0.4375
- expert_out_bias: bfloat16 [4, 768], P('exp'), may hold values from -3 to 3
Outputs:
- block_out: bfloat16 [64, 197, 768], P(('rep', 'exp'))
- input_grad: float32 [64, 197, 768], P(('rep', 'exp'))
- grad_attn_gain: float32 [768], P('exp')
- grad_attn_shift: float32 [768], P('exp')
- grad_qkv_weight: float32 [768, 2304], P('exp')
- grad_query_bias: float32 [768], P('exp')
- grad_value_bias: float32 [768], P('exp')
- grad_proj_weight: float32 [768, 768], P('exp')
- grad_proj_bias: float32 [768], P('exp')
- grad_moe_gain: float32 [768], P('exp')
- grad_moe_shift: float32 [768], P('exp')
- grad_router_weight: float32 [768, 4], P('exp')
- grad_expert_in: float32 [4, 768, 3072], P('exp')
- grad_expert_in_bias: float32 [4, 3072], P('exp')
- grad_expert_out: float32 [4, 3072, 768], P('exp')
- grad_expert_out_bias: float32 [4, 768], P('exp')
Inputs may be any that keep to these rules, and one draw needn't show every extreme that they name: `routes`: in the rows of one device, no expert is named by more than 264 tokens; the two experts of a token differ.
All inputs are finite; a program needn't handle non-finite values.
Results may differ from a plain program's by a relative error of at most 0.025.
Values may be sent and summed in bfloat16 or wider, within the bound.
A program may use at most 192 MiB of HBM per device.

v0:
```python
from functools import partial

import jax
import jax.numpy as jnp
from jax import lax
from jax.sharding import PartitionSpec as P

HEADS = 12
HEAD_DIM = 64


EPS = 1e-06


def normalize(values_in, gain_vec, shift_vec):
    row_mean = jnp.mean(values_in, axis=-1, keepdims=True)
    centered = values_in - row_mean
    inverse = lax.rsqrt(jnp.mean(centered * centered, axis=-1, keepdims=True) + EPS)
    normed = centered * inverse
    return (normed * gain_vec + shift_vec, normed, inverse)


def normalize_back(incoming, normed, inverse, gain_vec):
    scaled = incoming * gain_vec
    inner_mean = jnp.mean(scaled, axis=-1, keepdims=True)
    cross_mean = jnp.mean(scaled * normed, axis=-1, keepdims=True)
    back = inverse * (scaled - inner_mean - normed * cross_mean)
    return (back, jnp.sum(incoming * normed, axis=0), jnp.sum(incoming, axis=0))


def split_heads(block, image_count, seq_length):
    return block.reshape(image_count, seq_length, HEADS, HEAD_DIM)


def local(
    tokens,
    routes,
    cotangent,
    attn_gain,
    attn_shift,
    qkv_weight,
    query_bias,
    value_bias,
    proj_weight,
    proj_bias,
    moe_gain,
    moe_shift,
    router_weight,
    expert_in,
    expert_in_bias,
    expert_out,
    expert_out_bias,
):
    image_count, seq_length, model_width = tokens.shape
    row_count = image_count * seq_length
    expert_count = lax.axis_size("exp")
    capacity = min(row_count, (row_count * 8 // (3 * expert_count) + 7) // 8 * 8)
    score_scale = HEAD_DIM ** (-0.5)
    dense_shards = (
        attn_gain,
        attn_shift,
        qkv_weight,
        query_bias,
        value_bias,
        proj_weight,
        proj_bias,
        moe_gain,
        moe_shift,
        router_weight,
    )
    gathered = (
        lax.all_gather(dense_shards[0], "exp", axis=0, tiled=True),
        lax.all_gather(dense_shards[1], "exp", axis=0, tiled=True),
        lax.all_gather(dense_shards[2], "exp", axis=0, tiled=True),
        lax.all_gather(dense_shards[3], "exp", axis=0, tiled=True),
        lax.all_gather(dense_shards[4], "exp", axis=0, tiled=True),
        lax.all_gather(dense_shards[5], "exp", axis=0, tiled=True),
        lax.all_gather(dense_shards[6], "exp", axis=0, tiled=True),
        lax.all_gather(dense_shards[7], "exp", axis=0, tiled=True),
        lax.all_gather(dense_shards[8], "exp", axis=0, tiled=True),
        lax.all_gather(dense_shards[9], "exp", axis=0, tiled=True),
    )
    (
        gain_one,
        shift_one,
        qkv_full,
        query_add,
        value_add,
        proj_full,
        proj_add,
        gain_two,
        shift_two,
        router_full,
    ) = gathered
    gain_one = gain_one.astype(jnp.float32)
    gain_two = gain_two.astype(jnp.float32)
    source = tokens.reshape(row_count, model_width).astype(jnp.float32)
    first_out, normed_one, inverse_one = normalize(source, gain_one, shift_one.astype(jnp.float32))
    first_low = first_out.astype(jnp.bfloat16)
    qkv_bias = jnp.concatenate([query_add, jnp.zeros_like(query_add), value_add]).astype(
        jnp.float32
    )
    qkv_low = (jnp.dot(first_low, qkv_full, preferred_element_type=jnp.float32) + qkv_bias).astype(
        jnp.bfloat16
    )
    query_rows = split_heads(qkv_low[:, :model_width], image_count, seq_length)
    key_rows = split_heads(qkv_low[:, model_width : 2 * model_width], image_count, seq_length)
    value_rows = split_heads(qkv_low[:, 2 * model_width :], image_count, seq_length)
    scores = (
        jnp.einsum("ilhd,imhd->ihlm", query_rows, key_rows, preferred_element_type=jnp.float32)
        * score_scale
    )
    score_top = jnp.max(scores, axis=-1, keepdims=True)
    log_total = score_top + jnp.log(jnp.sum(jnp.exp(scores - score_top), axis=-1, keepdims=True))
    attn_probs = jnp.exp(scores - log_total)
    attended = (
        jnp.einsum(
            "ihlm,imhd->ilhd",
            attn_probs.astype(jnp.bfloat16),
            value_rows,
            preferred_element_type=jnp.float32,
        )
        .reshape(row_count, model_width)
        .astype(jnp.bfloat16)
    )
    branch = jnp.dot(attended, proj_full, preferred_element_type=jnp.float32) + proj_add.astype(
        jnp.float32
    )
    middle = source + branch
    second_out, normed_two, inverse_two = normalize(middle, gain_two, shift_two.astype(jnp.float32))
    second_low = second_out.astype(jnp.bfloat16)
    logits = jnp.dot(second_low, router_full, preferred_element_type=jnp.float32)
    router_probs = jax.nn.softmax(logits, axis=-1)
    route_ids = routes.reshape(row_count * 2)
    expert_ids = jnp.arange(expert_count, dtype=jnp.int32)
    one_hot = (route_ids[:, None] == expert_ids[None, :]).astype(jnp.int32)
    slot_ids = jnp.sum((jnp.cumsum(one_hot, axis=0) - one_hot) * one_hot, axis=1)
    chosen = one_hot.reshape(row_count, 2, expert_count).astype(jnp.float32)
    gates = jnp.sum(chosen * router_probs[:, None, :], axis=2)
    copies = jnp.repeat(second_low, 2, axis=0)
    empty_slots = jnp.zeros((expert_count, capacity, model_width), jnp.bfloat16)
    outgoing = empty_slots.at[route_ids, slot_ids].set(copies)
    arrived = lax.all_to_all(outgoing, "exp", split_axis=0, concat_axis=0, tiled=True)
    expert_rows = arrived.reshape(expert_count * capacity, model_width)
    pre_act = jnp.dot(
        expert_rows, expert_in[0], preferred_element_type=jnp.float32
    ) + expert_in_bias[0].astype(jnp.float32)
    hidden_low = jax.nn.gelu(pre_act, approximate=True).astype(jnp.bfloat16)
    result = (
        jnp.dot(hidden_low, expert_out[0], preferred_element_type=jnp.float32)
        + expert_out_bias[0].astype(jnp.float32)
    ).astype(jnp.bfloat16)
    returned = lax.all_to_all(
        result.reshape(expert_count, capacity, model_width),
        "exp",
        split_axis=0,
        concat_axis=0,
        tiled=True,
    )
    picked = returned[route_ids, slot_ids].astype(jnp.float32).reshape(row_count, 2, model_width)
    output = middle + jnp.sum(gates[:, :, None] * picked, axis=1)
    block_out = output.reshape(image_count, seq_length, model_width).astype(jnp.bfloat16)
    out_grad = cotangent.reshape(row_count, model_width).astype(jnp.float32)
    gate_grad = jnp.sum(out_grad[:, None, :] * picked, axis=2)
    row_grad = (
        (gates[:, :, None] * out_grad[:, None, :])
        .astype(jnp.bfloat16)
        .reshape(row_count * 2, model_width)
    )
    back_slots = empty_slots.at[route_ids, slot_ids].set(row_grad)
    result_grad = lax.all_to_all(
        back_slots, "exp", split_axis=0, concat_axis=0, tiled=True
    ).reshape(expert_count * capacity, model_width)
    grad_w_down = jnp.einsum(
        "rf,rd->fd", hidden_low, result_grad, preferred_element_type=jnp.float32
    )
    grad_down_bias = jnp.sum(result_grad.astype(jnp.float32), axis=0)
    hidden_grad = jnp.einsum(
        "rd,fd->rf", result_grad, expert_out[0], preferred_element_type=jnp.float32
    )
    _, gelu_back = jax.vjp(partial(jax.nn.gelu, approximate=True), pre_act)
    pre_grad = gelu_back(hidden_grad)[0].astype(jnp.bfloat16)
    grad_w_first = jnp.einsum(
        "rd,rf->df", expert_rows, pre_grad, preferred_element_type=jnp.float32
    )
    grad_first_bias = jnp.sum(pre_grad.astype(jnp.float32), axis=0)
    row_back = jnp.einsum(
        "rf,df->rd", pre_grad, expert_in[0], preferred_element_type=jnp.float32
    ).astype(jnp.bfloat16)
    came_back = lax.all_to_all(
        row_back.reshape(expert_count, capacity, model_width),
        "exp",
        split_axis=0,
        concat_axis=0,
        tiled=True,
    )
    copy_grad = (
        came_back[route_ids, slot_ids].astype(jnp.float32).reshape(row_count, 2, model_width)
    )
    prob_grad = jnp.sum(chosen * gate_grad[:, :, None], axis=1)
    logit_grad = router_probs * (
        prob_grad - jnp.sum(prob_grad * router_probs, axis=-1, keepdims=True)
    )
    logit_low = logit_grad.astype(jnp.bfloat16)
    grad_router = jnp.einsum("rd,re->de", second_low, logit_low, preferred_element_type=jnp.float32)
    norm_grad = jnp.sum(copy_grad, axis=1) + jnp.einsum(
        "re,de->rd", logit_low, router_full, preferred_element_type=jnp.float32
    )
    middle_part, grad_gain_two, grad_shift_two = normalize_back(
        norm_grad, normed_two, inverse_two, gain_two
    )
    middle_grad = out_grad + middle_part
    branch_low = middle_grad.astype(jnp.bfloat16)
    grad_proj = jnp.einsum("rd,re->de", attended, branch_low, preferred_element_type=jnp.float32)
    grad_proj_bias = jnp.sum(branch_low.astype(jnp.float32), axis=0)
    attended_grad = split_heads(
        jnp.einsum("re,de->rd", branch_low, proj_full, preferred_element_type=jnp.float32).astype(
            jnp.bfloat16
        ),
        image_count,
        seq_length,
    )
    scores = (
        jnp.einsum("ilhd,imhd->ihlm", query_rows, key_rows, preferred_element_type=jnp.float32)
        * score_scale
    )
    attn_probs = jnp.exp(scores - log_total)
    weight_grad = jnp.einsum(
        "ilhd,imhd->ihlm", attended_grad, value_rows, preferred_element_type=jnp.float32
    )
    value_grad = jnp.einsum(
        "ihlm,ilhd->imhd",
        attn_probs.astype(jnp.bfloat16),
        attended_grad,
        preferred_element_type=jnp.float32,
    )
    score_grad = (
        attn_probs * (weight_grad - jnp.sum(weight_grad * attn_probs, axis=-1, keepdims=True))
    ).astype(jnp.bfloat16)
    query_grad = (
        jnp.einsum("ihlm,imhd->ilhd", score_grad, key_rows, preferred_element_type=jnp.float32)
        * score_scale
    )
    key_grad = (
        jnp.einsum("ihlm,ilhd->imhd", score_grad, query_rows, preferred_element_type=jnp.float32)
        * score_scale
    )
    qkv_grad = jnp.concatenate(
        [
            query_grad.reshape(row_count, model_width),
            key_grad.reshape(row_count, model_width),
            value_grad.reshape(row_count, model_width),
        ],
        axis=1,
    ).astype(jnp.bfloat16)
    grad_qkv = jnp.einsum("rd,re->de", first_low, qkv_grad, preferred_element_type=jnp.float32)
    qkv_sums = jnp.sum(qkv_grad.astype(jnp.float32), axis=0)
    grad_query_add = qkv_sums[:model_width]
    grad_value_add = qkv_sums[2 * model_width :]
    first_grad = jnp.einsum("re,de->rd", qkv_grad, qkv_full, preferred_element_type=jnp.float32)
    source_part, grad_gain_one, grad_shift_one = normalize_back(
        first_grad, normed_one, inverse_one, gain_one
    )
    input_grad = (middle_grad + source_part).reshape(image_count, seq_length, model_width)
    expert_grads = (
        grad_w_first[None],
        grad_first_bias[None],
        grad_w_down[None],
        grad_down_bias[None],
    )
    dense_grads = (
        grad_gain_one,
        grad_shift_one,
        grad_qkv,
        grad_query_add,
        grad_value_add,
        grad_proj,
        grad_proj_bias,
        grad_gain_two,
        grad_shift_two,
        grad_router,
    )
    dense_owned = (
        lax.psum_scatter(dense_grads[0], "exp", scatter_dimension=0, tiled=True),
        lax.psum_scatter(dense_grads[1], "exp", scatter_dimension=0, tiled=True),
        lax.psum_scatter(dense_grads[2], "exp", scatter_dimension=0, tiled=True),
        lax.psum_scatter(dense_grads[3], "exp", scatter_dimension=0, tiled=True),
        lax.psum_scatter(dense_grads[4], "exp", scatter_dimension=0, tiled=True),
        lax.psum_scatter(dense_grads[5], "exp", scatter_dimension=0, tiled=True),
        lax.psum_scatter(dense_grads[6], "exp", scatter_dimension=0, tiled=True),
        lax.psum_scatter(dense_grads[7], "exp", scatter_dimension=0, tiled=True),
        lax.psum_scatter(dense_grads[8], "exp", scatter_dimension=0, tiled=True),
        lax.psum_scatter(dense_grads[9], "exp", scatter_dimension=0, tiled=True),
    )
    dense_summed = lax.psum(
        (
            dense_owned[0],
            dense_owned[1],
            dense_owned[2],
            dense_owned[3],
            dense_owned[4],
            dense_owned[5],
            dense_owned[6],
            dense_owned[7],
            dense_owned[8],
            dense_owned[9],
        ),
        "rep",
    )
    expert_summed = lax.psum(
        (expert_grads[0], expert_grads[1], expert_grads[2], expert_grads[3]), "rep"
    )
    return (
        block_out,
        input_grad,
        dense_summed[0],
        dense_summed[1],
        dense_summed[2],
        dense_summed[3],
        dense_summed[4],
        dense_summed[5],
        dense_summed[6],
        dense_summed[7],
        dense_summed[8],
        dense_summed[9],
        expert_summed[0],
        expert_summed[1],
        expert_summed[2],
        expert_summed[3],
    )


def solution(mesh):
    return jax.shard_map(
        local,
        mesh=mesh,
        in_specs=(
            P(("rep", "exp"), None, None),
            P(("rep", "exp"), None, None),
            P(("rep", "exp"), None, None),
            P("exp"),
            P("exp"),
            P("exp", None),
            P("exp"),
            P("exp"),
            P("exp", None),
            P("exp"),
            P("exp"),
            P("exp"),
            P("exp", None),
            P("exp", None, None),
            P("exp", None),
            P("exp", None, None),
            P("exp", None),
        ),
        out_specs=(
            P(("rep", "exp"), None, None),
            P(("rep", "exp"), None, None),
            P("exp"),
            P("exp"),
            P("exp", None),
            P("exp"),
            P("exp"),
            P("exp", None),
            P("exp"),
            P("exp"),
            P("exp"),
            P("exp", None),
            P("exp", None, None),
            P("exp", None),
            P("exp", None, None),
            P("exp", None),
        ),
        check_vma=False,
    )
```

profile of v0, /device:TPU:0, one launch (start us, length us, event | category | flops | bytes accessed | tf_op | source)
XLA Modules:
  0.0 1089.3 jit_solution(10497126717113553873)
XLA Ops:
  15.4 21.2 %all-reduce.18 = (bf16[768]{0:T(1024)(128)(2,1)S(1)}, bf16[768]{0:T(1024)(128)(2,1)S(1)}, bf16[768]{0:T(1024)(128)(2,1)S(1)}, bf16[768]{0:T(1024)(128)(2,1)S(1)}...) all-reduce(bf16[768]{0:T(1024)(128)(2,1)S(1)} %dynamic-update-slice, ...), channel_id=1, replica_groups=mesh['rep'=8,'exp'=4] {'exp'}, use_global_device_ids=true, to_apply=%add.4 | all-reduce | flops 5376 | bytes 21504
  38.7 43.9 %all-gather.4.cloned.1.call-done = bf16[768,2304]{1,0:T(8,128)(2,1)} async-done(((bf16[192,2304]{1,0:T(8,128)(2,1)}), bf16[768,2304]{1,0:T(8,128)(2,1)}) %all-gather.4.cloned.1.call-update) | async-done | bytes 3538960 | tf_op jit(solution)/shard_map/all_gather | solution.py:74
  82.6 3.7 fusion.13
  86.5 2.1 reshape.369
  88.5 2.2 copy.187
  90.8 2.1 reshape.370
  92.9 2.2 copy.185
  95.1 2.1 reshape.371
  97.2 3.1 copy.186
  100.3 2.0 multiply_reduce_fusion.1
  103.3 1.3 copy-done
  106.9 6.3 all-gather.6.cloned.1.call-done
  113.3 2.1 fusion.47
  116.7 1.6 broadcast_in_dim.16
  118.4 3.0 reshape.313
  122.6 114.4 %scatter_fusion = bf16[4,264,768]{2,1,0:T(8,128)(2,1)} fusion(bf16[4,264,768]{2,1,0:T(8,128)(2,1)} %broadcast_in_dim.15.clone, s32[788]{0:T(1024)S(1)} %get-tuple-element.123, bf16[788,768]{1,0:T(8,128)(2,1)S(1)} %reshape.313), kind=kCustom, calls=%fused_computation.2 | custom fusion | bytes 3637408 | tf_op jit(solution)/shard_map/scatter | solution.py:142
  237.1 4.5 all-to-all-start
  242.7 1.4 reshape.297
  244.2 2.3 mul.243
  246.4 4.1 mul.244
  250.6 34.4 %all-gather = bf16[4,192,4]{1,2,0:T(4,128)(2,1)S(1)} all-gather(bf16[1,192,4]{1,2,0:T(4,128)(2,1)S(1)} %bitcast.102), channel_id=1, replica_groups=mesh['rep'=8,'exp'=4] {'exp'}, dimensions={0}, use_global_device_ids=true | all-gather | bytes 7680 | tf_op jit(solution)/shard_map/all_gather | solution.py:81
  285.9 1.9 multiply_convert_fusion.2
  289.0 114.9 %scatter_fusion.1 = bf16[4,264,768]{2,1,0:T(8,128)(2,1)} fusion(bf16[4,264,768]{2,1,0:T(8,128)(2,1)} %broadcast_in_dim.15.clone.1, s32[788]{0:T(1024)S(1)} %get-tuple-element.123, bf16[788,768]{1,0:T(8,128)(2,1)S(1)} %multiply_convert_fusion.2), kind=kCustom, calls=%fused_computation.3 | custom fusion | bytes 3637408 | tf_op jit(solution)/shard_map/scatter | solution.py:170
  403.9 13.1 %all-to-all-start.2 = ((bf16[4,264,768]{2,1,0:T(8,128)(2,1)}), bf16[4,264,768]{2,1,0:T(8,128)(2,1)S(1)}, u32[]{:S(2)}, u32[]{:S(2)}) async-start(bf16[4,264,768]{2,1,0:T(8,128)(2,1)} %scatter_fusion.1), calls=%async_computation.2 | async-start | bytes 3244032 | tf_op jit(solution)/shard_map/all_to_all | solution.py:171
  417.1 10.2 convolution_add_fusion
  427.4 24.4 %all-to-all-done.2 = bf16[4,264,768]{2,1,0:T(8,128)(2,1)S(1)} async-done(((bf16[4,264,768]{2,1,0:T(8,128)(2,1)}), bf16[4,264,768]{2,1,0:T(8,128)(2,1)S(1)}, u32[]{:S(2)}, u32[]{:S(2)}) %all-to-all-start.2) | async-done | bytes 1622048 | tf_op jit(solution)/shard_map/all_to_all | solution.py:171
  451.8 17.1 %convert_reduce_fusion = (f32[3072]{0:T(1024)}, bf16[1056,3072]{1,0:T(8,128)(2,1)S(1)}) fusion(f32[1056,3072]{1,0:T(8,128)} %convolution_add_fusion, bf16[1056,768]{1,0:T(8,128)(2,1)S(1)} %bitcast.95, bf16[1,3072,768]{2,1,0:T(8,128)(2,1)} %param.32), kind=kOutput, calls=%fused_computation.14 | convolution fusion | flops 5054198784 | bytes 25817088 | tf_op jit(solution)/shard_map/rd,fd->rf/dot_general | solution.py:178
  468.9 11.0 %fusion.17 = bf16[1056,768]{1,0:T(8,128)(2,1)} fusion(bf16[1056,3072]{1,0:T(8,128)(2,1)S(1)} %get-tuple-element.173, bf16[1,768,3072]{2,1,0:T(8,128)(2,1)} %param.30), kind=kOutput, calls=%fused_computation.33 | convolution fusion | flops 4983644160 | bytes 12828672 | tf_op jit(solution)/shard_map/rf,df->rd/dot_general | solution.py:187
  479.9 3.6 all-to-all-start.3
  483.5 12.8 %fusion.20 = bf16[1056,768]{1,0:T(8,128)(2,1)} fusion(bf16[1,3072,768]{2,1,0:T(8,128)(2,1)} %param.32, f32[768]{0:T(1024)S(1)} %convert_reduce_fusion.5, f32[1056,3072]{1,0:T(8,128)} %convolution_add_fusion), kind=kOutput, calls=%fused_computation.34 | convolution fusion | flops 5013651456 | bytes 19319808 | tf_op jit(solution)/shard_map/dot_general | solution.py:150
  496.3 24.7 %all-to-all-done.3 = bf16[4,264,768]{2,1,0:T(8,128)(2,1)S(1)} async-done(((bf16[4,264,768]{2,1,0:T(8,128)(2,1)}), bf16[4,264,768]{2,1,0:T(8,128)(2,1)S(1)}, u32[]{:S(2)}, u32[]{:S(2)}) %all-to-all-start.3) | async-done | bytes 1622048 | tf_op jit(solution)/shard_map/all_to_all | solution.py:190
  521.0 3.6 all-to-all-start.1
  524.6 14.5 %gather_fusion.1 = bf16[788,768]{1,0:T(8,128)(2,1)} fusion(bf16[4,264,768]{2,1,0:T(8,128)(2,1)S(1)} %all-to-all-done.3, s32[788]{0:T(1024)S(1)} %get-tuple-element.122), kind=kCustom, calls=%fused_computation.1 | custom fusion | bytes 2427040 | tf_op jit(solution)/shard_map/gather | solution.py:198
  539.1 3.8 reshape.298
  543.0 19.1 %all-to-all-done.1 = bf16[4,264,768]{2,1,0:T(8,128)(2,1)S(1)} async-done(((bf16[4,264,768]{2,1,0:T(8,128)(2,1)}), bf16[4,264,768]{2,1,0:T(8,128)(2,1)S(1)}, u32[]{:S(2)}, u32[]{:S(2)}) %all-to-all-start.1) | async-done | bytes 1622048 | tf_op jit(solution)/shard_map/all_to_all | solution.py:153
  562.0 14.3 %gather_fusion = bf16[788,768]{1,0:T(8,128)(2,1)} fusion(bf16[4,264,768]{2,1,0:T(8,128)(2,1)S(1)} %all-to-all-done.1, s32[788]{0:T(1024)S(1)} %get-tuple-element.122), kind=kCustom, calls=%fused_computation | custom fusion | bytes 2427040 | tf_op jit(solution)/shard_map/gather | solution.py:160
  576.3 3.9 reshape.296
  580.3 8.4 multiply_reduce_fusion.2
  588.8 4.7 reduce_sum.246
  595.2 1.4 convert_reduce_fusion.3
  596.6 2.2 fusion.37
  599.5 2.1 reshape.372
  601.6 2.3 copy.199
  603.9 4.1 multiply_reduce_fusion
  609.8 1.7 copy.203
  611.5 3.3 reshape.288
  614.9 2.0 fusion.28
  618.1 3.4 fusion.26
  622.4 1.3 reshape.290
  624.9 1.4 copy-done.25
  626.3 5.1 fusion.42
  631.5 1.3 copy-done.21
  632.8 13.3 %convolution_bitcast_fusion = f32[1,3072,768]{2,1,0:T(8,128)} fusion(bf16[1056,768]{1,0:T(8,128)(2,1)S(1)} %bitcast.96, f32[1056,3072]{1,0:T(8,128)} %convolution_add_fusion), kind=kOutput, calls=%fused_computation.16 | convolution fusion | flops 5012029440 | bytes 24035328 | tf_op jit(solution)/shard_map/rf,rd->fd/dot_general | solution.py:174
  647.4 11.4 %convolution_bitcast_fusion.1 = f32[1,768,3072]{2,1,0:T(8,128)} fusion(bf16[1056,768]{1,0:T(8,128)(2,1)} %bitcast.4, bf16[1056,3072]{1,0:T(8,128)(2,1)} %copy-done.47), kind=kOutput, calls=%fused_computation.17 | convolution fusion | flops 4982833152 | bytes 17547264 | tf_op jit(solution)/shard_map/rd,rf->df/dot_general | solution.py:183
  658.8 112.1 %reduce-scatter.6.cloned.1.call-done = f32[192,2304]{1,0:T(8,128)} async-done(((f32[768,2304]{1,0:T(8,128)}), f32[192,2304]{1,0:T(8,128)}) %reduce-scatter.6.cloned.1.call-update) | async-done | bytes 1769488 | tf_op jit(solution)/shard_map/reduce_scatter | solution.py:286
  772.2 1.3 copy.210
  773.5 5.3 multiply_reduce_fusion.5
  779.3 1.6 copy.211
  781.7 18.3 %all-reduce.17 = (f32[768]{0:T(1024)S(1)}, f32[768]{0:T(1024)S(1)}, f32[768]{0:T(1024)S(1)}, f32[768]{0:T(1024)S(1)}, f32[768]{0:T(1024)S(1)}, /*index=5*/f32[768]{0:T(1024)S(1)}, f32[768]{0:T(1024)S(1)}) all-reduce(f32[768]{0:T(1024)S(1)} %get-tuple-element.114, ...), channel_id=2, replica_groups=mesh['rep'=8,'exp'=4] {'exp'}, use_global_device_ids=true, to_apply=%region_25.26.clone | all-reduce | flops 5376 | bytes 43008
  801.5 24.4 %all-reduce.15 = (f32[192]{0:T(256)}, f32[192]{0:T(256)}, f32[192]{0:T(256)}, f32[192]{0:T(256)}, f32[192]{0:T(256)}, /*index=5*/f32[192]{0:T(256)}, f32[192]{0:...) all-reduce(f32[192]{0:T(256)S(1)} %dynamic-slice.8, ...), channel_id=1, replica_groups=mesh['rep'=8,'exp'=4] {'rep'}, use_global_device_ids=true, to_apply=%region_26.27 | all-reduce | flops 5952 | bytes 47616 | tf_op jit(solution)/shard_map/psum | solution.py:295
  825.9 239.7 %all-reduce.21.cloned.1.call-done = (f32[192,2304]{1,0:T(8,128)}, f32[192,768]{1,0:T(8,128)}, f32[1,768,3072]{2,1,0:T(8,128)}, f32[1,3072,768]{2,1,0:T(8,128)}) async-done(((f32[192,2304]{1,0:T(8,128)}, f32[192,768]{1,0:T(8,128)}, f32[1,768,3072]{2,1,0:T(8,128)}, f32[1,3072,768]{2,1,0:T(8,128)}), (f32[192,2304]{1,0:T(8,128)}, f32[192,768]{1,0:T(8,128)}, f32[1,768,3072]{2,1,0:T(8,128)}, ...) | async-done | bytes 21233680 | tf_op jit(solution)/shard_map/psum | solution.py:295
  1065.6 2.9 copy.246
  1069.2 9.2 copy.248
  1078.5 3.7 copy.249
  (223 shorter events, 31.6 us)
Async XLA Ops:
  7.2 2.7 copy-start.22
  7.2 4.6 copy-start.32
  7.2 75.4 %all-gather.4.cloned.1.call-start = ((), (), s32[]{:S(2)}) async-start(), calls=%async_computation.7 | async-start | bytes 4423680 | tf_op jit(solution)/shard_map/all_gather | solution.py:74
  7.9 105.3 %all-gather.6.cloned.1.call-start = ((), (), s32[]{:S(2)}) async-start(), calls=%async_computation.8 | async-start | bytes 1474560 | tf_op jit(solution)/shard_map/all_gather | solution.py:77
  9.9 2.5 copy-start.39
  9.9 3.9 copy-start.40
  9.9 4.1 copy-start.41
  9.9 4.3 copy-start.42
  9.9 4.6 copy-start.43
  9.9 4.8 copy-start.44
  9.9 5.0 copy-start.45
  9.9 5.2 copy-start.46
  12.3 100.9 %copy-start.8 = (f32[394,768]{1,0:T(8,128)}, f32[394,768]{1,0:T(8,128)S(1)}, u32[]{:S(2)}) copy-start(f32[394,768]{1,0:T(8,128)S(1)} %reshape.292) | copy-start | bytes 3631108
  36.6 49.7 %copy-start.35 = (f32[768]{0:T(1024)}, f32[768]{0:T(1024)S(1)}, u32[]{:S(2)}) copy-start(f32[768]{0:T(1024)S(1)} %convert_element_type.148) | copy-start | bytes 9220
  90.8 12.6 %copy-start.12 = (bf16[2,197,12,64]{1,3,2,0:T(8,128)(2,1)}, bf16[2,197,12,64]{1,3,2,0:T(8,128)(2,1)S(1)}, u32[]{:S(2)}) copy-start(bf16[2,197,12,64]{1,3,2,0:T(8,128)(2,1)S(1)} %copy.187) | copy-start | bytes 1815556
  95.1 7.3 copy-start.16
  102.4 2.3 copy-start
  106.9 8.7 copy-start.18
  115.4 1.1 copy-start.1
  116.7 168.5 %copy-start.10 = (bf16[394,768]{1,0:T(8,128)(2,1)}, bf16[394,768]{1,0:T(8,128)(2,1)S(1)}, u32[]{:S(2)}) copy-start(bf16[394,768]{1,0:T(8,128)(2,1)S(1)} %add_convert_fusion.1) | copy-start | bytes 1815556
  237.1 4.5 copy-start.30
  237.1 166.8 %all-to-all-start = ((bf16[4,264,768]{2,1,0:T(8,128)(2,1)}), bf16[4,264,768]{2,1,0:T(8,128)(2,1)}, u32[]{:S(2)}, u32[]{:S(2)}) async-start(bf16[4,264,768]{2,1,0:T(8,128)(2,1)} %scatter_fusion), calls=%async_computation | async-start | bytes 3244032 | tf_op jit(solution)/shard_map/all_to_all | solution.py:143
  244.1 6.4 copy-start.5
  246.4 4.1 copy-start.38
  403.9 13.1 %copy-start.33 = (bf16[1,3072]{1,0:T(2,128)(2,1)S(1)}, bf16[1,3072]{1,0:T(2,128)(2,1)}, u32[]{:S(2)}) copy-start(bf16[1,3072]{1,0:T(2,128)(2,1)} %param.31) | copy-start | bytes 18436
  403.9 13.2 %copy-start.37 = (bf16[1,768]{1,0:T(2,128)(2,1)S(1)}, bf16[1,768]{1,0:T(2,128)(2,1)}, u32[]{:S(2)}) copy-start(bf16[1,768]{1,0:T(2,128)(2,1)} %param.33) | copy-start | bytes 4612
  403.9 47.9 %all-to-all-start.2 = ((bf16[4,264,768]{2,1,0:T(8,128)(2,1)}), bf16[4,264,768]{2,1,0:T(8,128)(2,1)S(1)}, u32[]{:S(2)}, u32[]{:S(2)}) async-start(bf16[4,264,768]{2,1,0:T(8,128)(2,1)} %scatter_fusion.1), calls=%async_computation.2 | async-start | bytes 3244032 | tf_op jit(solution)/shard_map/all_to_all | solution.py:171
  451.8 17.1 %copy-start.20 = (bf16[4,264,768]{2,1,0:T(8,128)(2,1)}, bf16[4,264,768]{2,1,0:T(8,128)(2,1)S(1)}, u32[]{:S(2)}) copy-start(bf16[4,264,768]{2,1,0:T(8,128)(2,1)S(1)} %all-to-all-done.2) | copy-start | bytes 4866052
  468.9 11.0 %copy-start.47 = (bf16[1056,3072]{1,0:T(8,128)(2,1)}, bf16[1056,3072]{1,0:T(8,128)(2,1)S(1)}, u32[]{:S(2)}) copy-start(bf16[1056,3072]{1,0:T(8,128)(2,1)S(1)} %get-tuple-element.173) | copy-start | bytes 19464196
  479.9 41.1 %all-to-all-start.3 = ((bf16[4,264,768]{2,1,0:T(8,128)(2,1)}), bf16[4,264,768]{2,1,0:T(8,128)(2,1)S(1)}, u32[]{:S(2)}, u32[]{:S(2)}) async-start(bf16[4,264,768]{2,1,0:T(8,128)(2,1)} %bitcast.10), calls=%async_computation.3 | async-start | bytes 3244032 | tf_op jit(solution)/shard_map/all_to_all | solution.py:190
  521.0 41.0 %all-to-all-start.1 = ((bf16[4,264,768]{2,1,0:T(8,128)(2,1)}), bf16[4,264,768]{2,1,0:T(8,128)(2,1)S(1)}, u32[]{:S(2)}, u32[]{:S(2)}) async-start(bf16[4,264,768]{2,1,0:T(8,128)(2,1)} %bitcast.97), calls=%async_computation.1 | async-start | bytes 3244032 | tf_op jit(solution)/shard_map/all_to_all | solution.py:153
  524.6 134.2 %reduce-scatter.8.cloned.1.call-start = ((), (), s32[]{:S(2)}) async-start(), calls=%async_computation.10 | async-start | bytes 2949120 | tf_op jit(solution)/shard_map/reduce_scatter | solution.py:289
  576.3 3.9 copy-start.6
  588.7 4.9 copy-start.2
  593.5 1.3 copy-start.7
  593.5 1.7 copy-start.23
  595.2 1.4 copy-start.19
  596.6 2.2 copy-start.3
  596.6 2.2 copy-start.24
  598.8 172.2 %reduce-scatter.6.cloned.1.call-start = ((), (), s32[]{:S(2)}) async-start(), calls=%async_computation.9 | async-start | bytes 8847360 | tf_op jit(solution)/shard_map/reduce_scatter | solution.py:286
  599.5 4.4 copy-start.13
  601.6 6.4 slice-start
  603.9 4.1 copy-start.14
  603.9 4.1 slice-start.1
  608.1 1.1 copy-start.17
  616.9 1.3 copy-start.15
  621.6 2.1 copy-start.27
  623.7 1.1 copy-start.28
  623.7 2.6 copy-start.9
  623.7 2.6 copy-start.36
  624.9 1.4 copy-start.25
  631.4 1.4 copy-start.21
  631.4 14.7 %copy-start.11 = (bf16[394,768]{1,0:T(8,128)(2,1)S(1)}, bf16[394,768]{1,0:T(8,128)(2,1)}, u32[]{:S(2)}) copy-start(bf16[394,768]{1,0:T(8,128)(2,1)} %copy-done.10) | copy-start | bytes 1815556
  631.4 169.1 %reduce-scatter.10.cloned.1.call-start = ((), (), s32[]{:S(2)}) async-start(), calls=%async_computation.11 | async-start | bytes 491520
  647.4 418.2 %all-reduce.21.cloned.1.call-start = ((), (), s32[]{:S(2)}) async-start(), calls=%async_computation.12 | async-start | bytes 42467328 | tf_op jit(solution)/shard_map/psum | solution.py:295
  771.0 1.1 copy-start.29
  773.5 5.3 copy-start.4
  779.3 2.0 copy-start.26
  779.3 22.2 %copy-start.34 = (f32[3072]{0:T(1024)S(1)}, f32[3072]{0:T(1024)}, u32[]{:S(2)}) copy-start(f32[3072]{0:T(1024)} %get-tuple-element.172) | copy-start | bytes 36868
  1065.5 2.9 copy-start.31
  1068.4 10.0 slice-start.2
  1069.2 9.2 slice-start.3
  1069.2 9.2 slice-start.4
Sparse Core Ops, SparseCore 0:
  9.6 72.9 all-gather.3
  84.2 29.0 all-gather.5
  598.9 46.8 reduce-scatter.7
  647.9 122.9 reduce-scatter.5
  773.7 21.3 reduce-scatter.9
  800.3 265.1 all-reduce.20
where the time goes:
time: 1100 us; the launch traced here: 1090 us
  waiting for transfers between devices  472 us (43%)
  local copies, waits for them, and re-layouts  344 us (31%)
  matrix products  110 us (10%)
  blocking collectives  98.2 us (9%)
  starting transfers between devices  25 us (2%)
  other arithmetic  23.5 us (2%)
  between operations  16.7 us (2%)
    psum x1, waiting for transfers between devices, local(): lax.psum((dense_owned[0], dense_owned[1], dense_owned[2], dense_owned[3],...  240 us
    scatter x1, local copies, waits for them, and re-layouts, local(): back_slots = empty_slots.at[route_ids, slot_ids].set(row_grad)  115 us
    scatter x1, local copies, waits for them, and re-layouts, local(): outgoing = empty_slots.at[route_ids, slot_ids].set(copies)  114 us
    reduce_scatter x1, waiting for transfers between devices, local(): lax.psum_scatter(dense_grads[2], 'exp', scatter_dimension=0, tiled=True)  112 us
    all_gather x1, waiting for transfers between devices, local(): lax.all_gather(dense_shards[2], 'exp', axis=0, tiled=True)  43.9 us
    unnamed x2, blocking collectives  39.5 us
    all_gather x1, blocking collectives, local(): lax.all_gather(dense_shards[9], 'exp', axis=0, tiled=True)  34.4 us
    unnamed x144, local copies, waits for them, and re-layouts  31 us
  transfers between devices with their start and end apart: 10, of which 7 were waited for; matrix products, arithmetic and copies ran while one was open for 25% of the time, Pallas kernels for 0%

commit v1 on v0

v1 whole, which is shorter than its diff:
```python
from functools import partial

import jax
import jax.numpy as jnp
from jax import lax
from jax.sharding import PartitionSpec as P

HEADS = 12
HEAD_DIM = 64


EPS = 1e-06


def normalize(values_in, gain_vec, shift_vec):
    row_mean = jnp.mean(values_in, axis=-1, keepdims=True)
    centered = values_in - row_mean
    inverse = lax.rsqrt(jnp.mean(centered * centered, axis=-1, keepdims=True) + EPS)
    normed = centered * inverse
    return (normed * gain_vec + shift_vec, normed, inverse)


def normalize_back(incoming, normed, inverse, gain_vec):
    scaled = incoming * gain_vec
    inner_mean = jnp.mean(scaled, axis=-1, keepdims=True)
    cross_mean = jnp.mean(scaled * normed, axis=-1, keepdims=True)
    back = inverse * (scaled - inner_mean - normed * cross_mean)
    return (back, jnp.sum(incoming * normed, axis=0), jnp.sum(incoming, axis=0))


def split_heads(block, image_count, seq_length):
    return block.reshape(image_count, seq_length, HEADS, HEAD_DIM)


def gather_params(packed):
    share = packed.shape[0] // lax.axis_size("rep")
    mine = lax.dynamic_slice_in_dim(packed, lax.axis_index("rep") * share, share, 0)
    across = lax.all_gather(mine, "exp", axis=0, tiled=False)
    return lax.all_gather(across, "rep", axis=1, tiled=False).reshape(-1, packed.shape[1])


def local(
    tokens,
    routes,
    cotangent,
    attn_gain,
    attn_shift,
    qkv_weight,
    query_bias,
    value_bias,
    proj_weight,
    proj_bias,
    moe_gain,
    moe_shift,
    router_weight,
    expert_in,
    expert_in_bias,
    expert_out,
    expert_out_bias,
):
    image_count, seq_length, model_width = tokens.shape
    row_count = image_count * seq_length
    expert_count = lax.axis_size("exp")
    capacity = min(row_count, (row_count * 8 // (3 * expert_count) + 7) // 8 * 8)
    score_scale = HEAD_DIM ** (-0.5)
    own = lax.axis_index("exp")
    low = jnp.bfloat16
    wide = jnp.float32
    pair = routes.reshape(row_count, 2)
    expert_ids = jnp.arange(expert_count, dtype=jnp.int32)
    named = pair[:, :, None] == expert_ids[None, None, :]
    member = jnp.sum(named.astype(jnp.int32), axis=1)
    earlier = (
        jnp.arange(row_count)[:, None] > jnp.arange(row_count)[None, :]
    ).astype(low)
    slots = jnp.dot(earlier, member.astype(low), preferred_element_type=wide).astype(jnp.int32)
    place = jnp.sum(
        named * (slots + expert_ids[None, :] * capacity)[:, None, :], axis=2
    )
    slot_total = expert_count * capacity
    all_slots = jnp.arange(slot_total, dtype=jnp.int32)
    chosen = named.astype(wide)
    pick_0 = (place[:, 0][:, None] == all_slots[None, :]).astype(low)
    pick_1 = (place[:, 1][:, None] == all_slots[None, :]).astype(low)
    pick_both = pick_0 + pick_1

    def send_out(rows):
        filled = lax.dot_general(
            pick_both, rows, (((0,), (0,)), ((), ())), preferred_element_type=wide
        ).astype(low)
        return exchange(filled)

    def exchange(filled):
        return lax.all_to_all(
            filled.reshape(expert_count, capacity, model_width),
            "exp",
            split_axis=0,
            concat_axis=0,
            tiled=True,
        ).reshape(slot_total, model_width)

    vector_width = 128
    columns = jnp.concatenate(
        [
            jnp.stack(
                [
                    attn_gain,
                    attn_shift,
                    query_bias,
                    value_bias,
                    proj_bias,
                    moe_gain,
                    moe_shift,
                ],
                axis=1,
            ),
            router_weight,
        ],
        axis=1,
    )
    columns = jnp.pad(columns, ((0, 0), (0, vector_width - columns.shape[1])))
    packed = jnp.concatenate([qkv_weight, proj_weight, columns], axis=1)
    full = gather_params(packed)
    qkv_full = full[:, : 3 * model_width]
    proj_full = full[:, 3 * model_width : 4 * model_width]
    vectors = full[:, 4 * model_width :]
    router_full = vectors[:, 7 : 7 + expert_count]
    vector_rows = vectors[:, :7].T.astype(wide)
    gain_one = vector_rows[0]
    shift_one = vector_rows[1]
    query_add = vector_rows[2]
    value_add = vector_rows[3]
    proj_add = vector_rows[4]
    gain_two = vector_rows[5]
    shift_two = vector_rows[6]

    cotangent_rows = cotangent.reshape(row_count, model_width)
    slot_cotangent = send_out(cotangent_rows)

    source = tokens.reshape(row_count, model_width).astype(wide)
    first_out, normed_one, inverse_one = normalize(source, gain_one, shift_one)
    first_low = first_out.astype(low)
    qkv_bias = jnp.concatenate([query_add, jnp.zeros_like(query_add), value_add])
    qkv_low = (jnp.dot(first_low, qkv_full, preferred_element_type=wide) + qkv_bias).astype(low)
    query_rows = split_heads(qkv_low[:, :model_width], image_count, seq_length)
    key_rows = split_heads(qkv_low[:, model_width : 2 * model_width], image_count, seq_length)
    value_rows = split_heads(qkv_low[:, 2 * model_width :], image_count, seq_length)
    scores = (
        jnp.einsum("ilhd,imhd->ihlm", query_rows, key_rows, preferred_element_type=wide)
        * score_scale
    )
    score_top = jnp.max(scores, axis=-1, keepdims=True)
    log_total = score_top + jnp.log(jnp.sum(jnp.exp(scores - score_top), axis=-1, keepdims=True))
    attn_probs = jnp.exp(scores - log_total)
    attended = (
        jnp.einsum(
            "ihlm,imhd->ilhd", attn_probs.astype(low), value_rows, preferred_element_type=wide
        )
        .reshape(row_count, model_width)
        .astype(low)
    )
    branch = jnp.dot(attended, proj_full, preferred_element_type=wide) + proj_add
    middle = source + branch
    second_out, normed_two, inverse_two = normalize(middle, gain_two, shift_two)
    second_low = second_out.astype(low)
    expert_rows = send_out(second_low)

    logits = jnp.dot(second_low, router_full, preferred_element_type=wide)
    router_probs = jax.nn.softmax(logits, axis=-1)
    gates = jnp.sum(chosen * router_probs[:, None, :], axis=2)

    slot_probs = jax.nn.softmax(
        jnp.dot(expert_rows, router_full, preferred_element_type=wide), axis=-1
    )
    slot_gates = jnp.sum(
        jnp.where(expert_ids[None, :] == own, slot_probs, 0.0), axis=1, keepdims=True
    )
    result_grad = (slot_gates * slot_cotangent.astype(wide)).astype(low)
    pre_act = jnp.dot(expert_rows, expert_in[0], preferred_element_type=wide) + expert_in_bias[
        0
    ].astype(wide)
    hidden_low = jax.nn.gelu(pre_act, approximate=True).astype(low)
    result = (
        jnp.dot(hidden_low, expert_out[0], preferred_element_type=wide)
        + expert_out_bias[0].astype(wide)
    ).astype(low)
    returned = exchange(result)
    hidden_grad = jnp.einsum("rd,fd->rf", result_grad, expert_out[0], preferred_element_type=wide)
    _, gelu_back = jax.vjp(partial(jax.nn.gelu, approximate=True), pre_act)
    pre_grad = gelu_back(hidden_grad)[0].astype(low)
    row_back = jnp.einsum("rf,df->rd", pre_grad, expert_in[0], preferred_element_type=wide).astype(
        low
    )
    came_back = exchange(row_back)
    grad_w_down = jnp.einsum(
        "rf,rd->fd", hidden_low, result_grad, preferred_element_type=wide
    ).astype(low)
    grad_down_bias = jnp.sum(result_grad.astype(wide), axis=0)
    grad_w_first = jnp.einsum(
        "rd,rf->df", expert_rows, pre_grad, preferred_element_type=wide
    ).astype(low)
    grad_first_bias = jnp.sum(pre_grad.astype(wide), axis=0)
    grad_w_first, grad_w_down = lax.psum((grad_w_first, grad_w_down), "rep")

    picked_0 = jnp.dot(pick_0, returned, preferred_element_type=wide)
    picked_1 = jnp.dot(pick_1, returned, preferred_element_type=wide)
    output = middle + gates[:, 0:1] * picked_0 + gates[:, 1:2] * picked_1
    block_out = output.reshape(image_count, seq_length, model_width).astype(low)
    out_grad = cotangent_rows.astype(wide)
    gate_grad_0 = jnp.sum(out_grad * picked_0, axis=1, keepdims=True)
    gate_grad_1 = jnp.sum(out_grad * picked_1, axis=1, keepdims=True)
    prob_grad = chosen[:, 0] * gate_grad_0 + chosen[:, 1] * gate_grad_1
    logit_grad = router_probs * (
        prob_grad - jnp.sum(prob_grad * router_probs, axis=-1, keepdims=True)
    )
    logit_low = logit_grad.astype(low)
    grad_router = jnp.einsum("rd,re->de", second_low, logit_low, preferred_element_type=wide)
    norm_grad = jnp.dot(pick_both, came_back, preferred_element_type=wide) + jnp.einsum(
        "re,de->rd", logit_low, router_full, preferred_element_type=wide
    )
    middle_part, grad_gain_two, grad_shift_two = normalize_back(
        norm_grad, normed_two, inverse_two, gain_two
    )
    middle_grad = out_grad + middle_part
    branch_low = middle_grad.astype(low)
    grad_proj = jnp.einsum("rd,re->de", attended, branch_low, preferred_element_type=wide)
    grad_proj_bias = jnp.sum(branch_low.astype(wide), axis=0)
    attended_grad = split_heads(
        jnp.einsum("re,de->rd", branch_low, proj_full, preferred_element_type=wide).astype(low),
        image_count,
        seq_length,
    )
    weight_grad = jnp.einsum(
        "ilhd,imhd->ihlm", attended_grad, value_rows, preferred_element_type=wide
    )
    value_grad = jnp.einsum(
        "ihlm,ilhd->imhd", attn_probs.astype(low), attended_grad, preferred_element_type=wide
    )
    score_grad = (
        attn_probs * (weight_grad - jnp.sum(weight_grad * attn_probs, axis=-1, keepdims=True))
    ).astype(low)
    query_grad = (
        jnp.einsum("ihlm,imhd->ilhd", score_grad, key_rows, preferred_element_type=wide)
        * score_scale
    )
    key_grad = (
        jnp.einsum("ihlm,ilhd->imhd", score_grad, query_rows, preferred_element_type=wide)
        * score_scale
    )
    qkv_grad = jnp.concatenate(
        [
            query_grad.reshape(row_count, model_width),
            key_grad.reshape(row_count, model_width),
            value_grad.reshape(row_count, model_width),
        ],
        axis=1,
    ).astype(low)
    grad_qkv = jnp.einsum("rd,re->de", first_low, qkv_grad, preferred_element_type=wide)
    qkv_sums = jnp.sum(qkv_grad.astype(wide), axis=0)
    first_grad = jnp.einsum("re,de->rd", qkv_grad, qkv_full, preferred_element_type=wide)
    source_part, grad_gain_one, grad_shift_one = normalize_back(
        first_grad, normed_one, inverse_one, gain_one
    )
    input_grad = (middle_grad + source_part).reshape(image_count, seq_length, model_width)

    owned_rows = model_width // expert_count
    bias_columns = (grad_first_bias.shape[0] + model_width) // owned_rows
    own_bias = jnp.concatenate([grad_first_bias, grad_down_bias]).reshape(bias_columns, owned_rows)
    own_bias = jnp.tile(own_bias.T, (expert_count, 1))
    is_own = (jnp.arange(model_width) // owned_rows == own)[:, None]
    vector_grads = jnp.concatenate(
        [
            jnp.stack(
                [
                    grad_gain_one,
                    grad_shift_one,
                    qkv_sums[:model_width],
                    qkv_sums[2 * model_width :],
                    grad_proj_bias,
                    grad_gain_two,
                    grad_shift_two,
                ],
                axis=1,
            ),
            grad_router,
            jnp.where(is_own, own_bias, 0.0),
        ],
        axis=1,
    )
    vector_grads = jnp.pad(vector_grads, ((0, 0), (0, vector_width - vector_grads.shape[1])))
    dense_packed = jnp.concatenate([grad_qkv, grad_proj, vector_grads], axis=1).astype(low)
    dense_owned = lax.psum_scatter(dense_packed, "exp", scatter_dimension=0, tiled=True)
    dense_owned, grad_w_first, grad_w_down = lax.optimization_barrier(
        (dense_owned, grad_w_first, grad_w_down)
    )
    dense_summed = lax.psum(dense_owned, "rep").astype(wide)
    summed_vectors = dense_summed[:, 4 * model_width :]
    summed_rows = summed_vectors.T
    router_end = 7 + expert_count
    summed_bias = summed_rows[router_end : router_end + bias_columns].reshape(
        1, bias_columns * owned_rows
    )
    first_width = grad_first_bias.shape[0]
    return (
        block_out,
        input_grad,
        summed_rows[0],
        summed_rows[1],
        dense_summed[:, : 3 * model_width],
        summed_rows[2],
        summed_rows[3],
        dense_summed[:, 3 * model_width : 4 * model_width],
        summed_rows[4],
        summed_rows[5],
        summed_rows[6],
        summed_vectors[:, 7:router_end],
        grad_w_first.astype(wide)[None],
        summed_bias[:, :first_width],
        grad_w_down.astype(wide)[None],
        summed_bias[:, first_width:],
    )


def solution(mesh):
    return jax.shard_map(
        local,
        mesh=mesh,
        in_specs=(
            P(("rep", "exp"), None, None),
            P(("rep", "exp"), None, None),
            P(("rep", "exp"), None, None),
            P("exp"),
            P("exp"),
            P("exp", None),
            P("exp"),
            P("exp"),
            P("exp", None),
            P("exp"),
            P("exp"),
            P("exp"),
            P("exp", None),
            P("exp", None, None),
            P("exp", None),
            P("exp", None, None),
            P("exp", None),
        ),
        out_specs=(
            P(("rep", "exp"), None, None),
            P(("rep", "exp"), None, None),
            P("exp"),
            P("exp"),
            P("exp", None),
            P("exp"),
            P("exp"),
            P("exp", None),
            P("exp"),
            P("exp"),
            P("exp"),
            P("exp", None),
            P("exp", None, None),
            P("exp", None),
            P("exp", None, None),
            P("exp", None),
        ),
        check_vma=False,
    )
```

time: 1100 us -> 566 us (0.51)
  local copies, waits for them, and re-layouts: 344 us -> 65.7 us
  waiting for transfers between devices: 472 us -> 288 us
  blocking collectives: 98.2 us -> 18.7 us
  matrix products: 110 us -> 122 us
    scatter x2 -> x0, local copies, waits for them, and re-layouts: 229 us -> none  [the longest x1 115 us: local(): back_slots = empty_slots.at[route_ids, slot_ids].set(row_grad)]
    psum x1 -> x2, waiting for transfers between devices: 240 us -> 101 us  [the longest x1 51.8 us: local(): grad_w_first, grad_w_down = lax.psum((grad_w_first, grad_w_down), 'rep')]
    unnamed x2 -> x0, blocking collectives: 39.5 us -> none
    gather x2 -> x0, local copies, waits for them, and re-layouts: 28.8 us -> none  [the longest x1 14.5 us: local(): came_back[route_ids, slot_ids].astype(jnp.float32)]
    psum x1 -> x0, blocking collectives: 24.4 us -> none  [local(): lax.psum((dense_owned[0], dense_owned[1], dense_owned[2], dense_owned[3],...]
    reduce_scatter x2 -> x1, waiting for transfers between devices: 112 us -> 91.6 us  [local(): lax.psum_scatter(dense_packed, 'exp', scatter_dimension=0, tiled=True)]
    all_gather x1, blocking collectives: 34.4 us -> 18.7 us  [gather_params(): across = lax.all_gather(mine, 'exp', axis=0, tiled=False)]
    unnamed x144 -> x104, local copies, waits for them, and re-layouts: 31 us -> 16.7 us
  transfers between devices with their start and end apart: 10 -> 8, of which waited for: 7 -> 7; matrix products, arithmetic and copies ran while one was open for 25% -> 29% of each run, Pallas kernels for 0% -> 0%
where the time goes in v1:
time: 566 us; the launch traced here: 559 us
  waiting for transfers between devices  288 us (51%)
  matrix products  122 us (22%)
  local copies, waits for them, and re-layouts  65.7 us (12%)
  other arithmetic  30.8 us (5%)
  starting transfers between devices  18.7 us (3%)
  blocking collectives  18.7 us (3%)
  between operations  15.2 us (3%)
    reduce_scatter x1, waiting for transfers between devices, local(): lax.psum_scatter(dense_packed, 'exp', scatter_dimension=0, tiled=True)  91.6 us
    all_to_all x4, waiting for transfers between devices, exchange(): lax.all_to_all(filled.reshape(expert_count, capacity, model_width), 'exp'...  59.1 us
    psum x1, waiting for transfers between devices, local(): grad_w_first, grad_w_down = lax.psum((grad_w_first, grad_w_down), 'rep')  51.8 us
    psum x1, waiting for transfers between devices, local(): dense_summed = lax.psum(dense_owned, 'rep').astype(wide)  49 us
    all_gather x1, waiting for transfers between devices, gather_params(): lax.all_gather(across, 'rep', axis=1, tiled=False)  36.4 us
    all_gather x1, blocking collectives, gather_params(): across = lax.all_gather(mine, 'exp', axis=0, tiled=False)  18.7 us
    all_to_all x4, starting transfers between devices, exchange(): lax.all_to_all(filled.reshape(expert_count, capacity, model_width), 'exp'...  18.3 us
    reshape x8, local copies, waits for them, and re-layouts, split_heads(): return block.reshape(image_count, seq_length, HEADS, HEAD_DIM)  18.2 us
  transfers between devices with their start and end apart: 8, of which 7 were waited for; matrix products, arithmetic and copies ran while one was open for 29% of the time, Pallas kernels for 0%

profile of v1, /device:TPU:0, one launch (start us, length us, event | category | flops | bytes accessed | tf_op | source)
XLA Modules:
  0.0 559.3 jit_solution(1639865696222738483)
XLA Ops:
  13.8 18.7 %all-gather = bf16[96,3200]{1,0:T(8,128)(2,1)} all-gather(bf16[24,3200]{1,0:T(8,128)(2,1)S(1)} %fusion.61), channel_id=2, replica_groups=mesh['rep'=8,'exp'=4] {'exp'}, dimensions={0}, use_global_device_ids=true | all-gather | bytes 768000 | tf_op jit(solution)/shard_map/all_gather | solution.py:38
  35.8 1.4 reshape.241
  37.6 36.4 %all-gather.4.cloned.1.call-done = bf16[4,192,3200]{2,1,0:T(8,128)(2,1)} async-done(((bf16[4,24,3200]{2,1,0:T(8,128)(2,1)}), bf16[4,192,3200]{2,1,0:T(8,128)(2,1)}) %all-gather.4.cloned.1.call-update) | async-done | bytes 4915216 | tf_op jit(solution)/shard_map/all_gather | solution.py:39
  75.0 1.4 slice_reduce_fusion.1
  77.0 3.7 fusion.15
  80.8 2.1 reshape.252
  82.9 3.1 copy.173
  86.0 2.1 reshape.251
  88.1 2.2 copy.172
  90.3 2.1 reshape.250
  92.4 2.2 copy.174
  94.6 2.3 multiply_reduce_fusion.1
  101.5 2.3 fusion.88
  104.4 2.4 convolution_convert_fusion.4
  106.9 4.7 all-to-all-start
  111.6 2.0 copy.178
  113.6 2.0 reshape.230
  117.3 3.5 convolution_convert_fusion.3
  120.8 1.3 fusion.90
  122.2 27.9 %all-to-all-done = bf16[4,264,768]{2,1,0:T(8,128)(2,1)S(1)} async-done(((bf16[4,264,768]{2,1,0:T(8,128)(2,1)}), bf16[4,264,768]{2,1,0:T(8,128)(2,1)S(1)}, u32[]{:S(2)}, u32[]{:S(2)}) %all-to-all-start) | async-done | bytes 1622048 | tf_op jit(solution)/shard_map/all_to_all | solution.py:94
  151.2 4.0 all-to-all-start.2
  155.2 2.0 fusion.89
  157.5 7.6 %convolution_add_fusion = f32[1056,3072]{1,0:T(8,128)S(1)} fusion(bf16[1056,768]{1,0:T(8,128)(2,1)} %bitcast.121, f32[3072]{0:T(1024)S(1)} %bitcast.140, bf16[1,768,3072]{2,1,0:T(8,128)(2,1)} %param.30), kind=kOutput, calls=%fused_computation.2 | convolution fusion | flops 4986077184 | bytes 19329024 | tf_op jit(solution)/shard_map/dot_general | solution.py:179
  165.1 4.6 copy-done.42
  169.7 11.0 %fusion.22 = bf16[1056,768]{1,0:T(8,128)(2,1)} fusion(bf16[1,3072,768]{2,1,0:T(8,128)(2,1)} %param.32, f32[768]{0:T(1024)S(1)} %copy-done.31, f32[1056,3072]{1,0:T(8,128)S(1)} %convolution_add_fusion), kind=kOutput, calls=%fused_computation.37 | convolution fusion | flops 5013651456 | bytes 19319808 | tf_op jit(solution)/shard_map/dot_general | solution.py:184
  180.7 12.1 %all-to-all-done.2 = bf16[4,264,768]{2,1,0:T(8,128)(2,1)S(1)} async-done(((bf16[4,264,768]{2,1,0:T(8,128)(2,1)}), bf16[4,264,768]{2,1,0:T(8,128)(2,1)S(1)}, u32[]{:S(2)}, u32[]{:S(2)}) %all-to-all-start.2) | async-done | bytes 1622048 | tf_op jit(solution)/shard_map/all_to_all | solution.py:94
  192.8 4.4 all-to-all-start.1
  197.6 16.0 %convert_reduce_fusion = (bf16[3072]{0:T(1024)(128)(2,1)S(1)}, bf16[1056,3072]{1,0:T(8,128)(2,1)S(1)}) fusion(f32[1056,3072]{1,0:T(8,128)} %copy-done.42, bf16[1056,768]{1,0:T(8,128)(2,1)S(1)} %bitcast.138, bf16[1,3072,768]{2,1,0:T(8,128)(2,1)} %param.32), kind=kOutput, calls=%fused_computation.10 | convolution fusion | flops 5054198784 | bytes 25810944 | tf_op jit(solution)/shard_map/rd,fd->rf/dot_general | solution.py:188
  213.9 14.7 %convolution_convert_fusion = bf16[3072,768]{1,0:T(8,128)(2,1)} fusion(bf16[1056,768]{1,0:T(8,128)(2,1)S(1)} %fusion.25, f32[1056,3072]{1,0:T(8,128)} %copy-done.42), kind=kOutput, calls=%fused_computation.14 | convolution fusion | flops 5014388736 | bytes 19316736 | tf_op jit(solution)/shard_map/rf,rd->fd/dot_general | solution.py:195
  228.6 8.9 %fusion.19 = bf16[1056,768]{1,0:T(8,128)(2,1)} fusion(bf16[1056,3072]{1,0:T(8,128)(2,1)S(1)} %get-tuple-element.158, bf16[1,768,3072]{2,1,0:T(8,128)(2,1)} %param.30), kind=kOutput, calls=%fused_computation.34 | convolution fusion | flops 4983644160 | bytes 12828672 | tf_op jit(solution)/shard_map/rf,df->rd/dot_general | solution.py:191
  237.5 5.2 all-to-all-start.3
  242.7 10.8 %convolution_convert_fusion.1 = bf16[768,3072]{1,0:T(8,128)(2,1)} fusion(bf16[1056,768]{1,0:T(8,128)(2,1)S(1)} %bitcast.122, bf16[1056,3072]{1,0:T(8,128)(2,1)} %copy-done.41), kind=kOutput, calls=%fused_computation.15 | convolution fusion | flops 4985192448 | bytes 12828672 | tf_op jit(solution)/shard_map/rd,rf->df/dot_general | solution.py:199
  254.4 2.5 fusion.30
  256.9 3.6 fusion.39
  260.6 19.2 %all-to-all-done.3 = bf16[4,264,768]{2,1,0:T(8,128)(2,1)} async-done(((bf16[4,264,768]{2,1,0:T(8,128)(2,1)}), bf16[4,264,768]{2,1,0:T(8,128)(2,1)}, u32[]{:S(2)}, u32[]{:S(2)}) %all-to-all-start.3) | async-done | bytes 1622048 | tf_op jit(solution)/shard_map/all_to_all | solution.py:94
  279.8 2.7 fusion.45
  282.5 2.8 multiply_reduce_fusion.2
  286.9 2.0 convolution_convert_fusion.8
  288.9 2.1 reshape.253
  291.0 2.4 copy.180
  293.4 3.4 fusion.36
  297.8 1.3 reshape.237
  299.1 4.1 multiply_reduce_fusion
  305.0 1.7 copy.184
  306.7 3.5 reshape.235
  310.2 2.0 fusion.38
  313.0 1.3 reshape.236
  314.4 1.3 constant_dynamic-update-slice_fusion.1
  315.9 6.2 %multiply_reduce_fusion.3 = (bf16[768]{0:T(1024)(128)(2,1)S(1)}, f32[394]{0:T(512)S(1)}, f32[394]{0:T(512)S(1)}, bf16[768]{0:T(1024)(128)(2,1)S(1)}, f32[394,768]{1,0:T(8,128)}) fusion(f32[394,768]{1,0:T(8,128)S(1)} %copy-done.5, f32[394]{0:T(512)S(1)} %copy-done.28, f32[394]{0:T(512)S(1)} %copy-done.26, f32[768]{0:T(1024)S(1)} %copy-done.23, ...), kind=kOutput, calls=%fused_computation.74 | convolution fusion | flops 1397064960 | bytes 7787680 | tf_op jit(solution)/shard_map/re,de->rd/dot_general | solution.py:260
  322.1 2.3 reduce.3
  325.2 2.1 convolution_convert_fusion.5
  327.3 2.3 convolution_convert_fusion.2
  329.6 2.6 fusion.8
  333.7 1.3 copy.194
  335.0 2.7 multiply_add_fusion
  337.8 1.4 reshape.238
  339.2 1.6 copy.195
  340.8 51.8 %all-reduce.8.cloned.1.call-done = (bf16[768,3072]{1,0:T(8,128)(2,1)}, bf16[3072,768]{1,0:T(8,128)(2,1)}) async-done(((bf16[768,3072]{1,0:T(8,128)(2,1)}, bf16[3072,768]{1,0:T(8,128)(2,1)}), (bf16[768,3072]{1,0:T(8,128)(2,1)}, bf16[3072,768]{1,0:T(8,128)(2,1)})) %all-reduce.8.cloned.1.call-update) | async-done | bytes 9437200 | tf_op jit(solution)/shard_map/psum | solution.py:203
  392.6 91.6 %reduce-scatter.2.cloned.1.call-done = bf16[192,3200]{1,0:T(8,128)(2,1)} async-done(((bf16[768,3200]{1,0:T(8,128)(2,1)}), bf16[192,3200]{1,0:T(8,128)(2,1)}) %reduce-scatter.2.cloned.1.call-update) | async-done | bytes 1228816 | tf_op jit(solution)/shard_map/reduce_scatter | solution.py:292
  484.2 7.5 %bitcast_convert_fusion.1 = f32[1,768,3072]{2,1,0:T(8,128)} fusion(bf16[768,3072]{1,0:T(8,128)(2,1)} %get-tuple-element.20), kind=kLoop, calls=%fused_computation.23 | loop fusion | flops 2359296 | bytes 14155776 | tf_op jit(solution)/shard_map/broadcast_in_dim | solution.py:317
  491.7 4.5 bitcast_convert_fusion
  496.2 49.0 %all-reduce.6.cloned.1.call-done = bf16[192,3200]{1,0:T(8,128)(2,1)} async-done(((bf16[192,3200]{1,0:T(8,128)(2,1)}), bf16[192,3200]{1,0:T(8,128)(2,1)}) %all-reduce.6.cloned.1.call-update) | async-done | bytes 1228816 | tf_op jit(solution)/shard_map/psum | solution.py:296
  545.2 1.5 convert_element_type.193
  550.9 1.3 slice.175
  (195 shorter events, 33.5 us)
Async XLA Ops:
  7.2 25.4 %copy-start.32 = (s32[2,197,2]{1,2,0:T(2,128)S(1)}, s32[2,197,2]{1,2,0:T(2,128)}, u32[]{:S(2)}) copy-start(s32[2,197,2]{1,2,0:T(2,128)} %param.18) | copy-start | bytes 9460
  7.2 25.4 %copy-start.14 = (bf16[2,197,768]{2,0,1:T(2,128)(2,1)S(1)}, bf16[2,197,768]{2,0,1:T(2,128)(2,1)}, u32[]{:S(2)}) copy-start(bf16[2,197,768]{2,0,1:T(2,128)(2,1)} %param.17) | copy-start | bytes 1815556
  7.2 66.8 %all-gather.4.cloned.1.call-start = ((), (), s32[]{:S(2)}) async-start(), calls=%async_computation.7 | async-start | bytes 5529600 | tf_op jit(solution)/shard_map/all_gather | solution.py:39
  34.5 41.9 %copy-start.25 = (f32[394]{0:T(512)}, f32[394]{0:T(512)S(1)}, u32[]{:S(2)}) copy-start(f32[394]{0:T(512)S(1)} %div.53) | copy-start | bytes 4732
  35.8 40.6 %copy-start.27 = (f32[394]{0:T(512)}, f32[394]{0:T(512)S(1)}, u32[]{:S(2)}) copy-start(f32[394]{0:T(512)S(1)} %rsqrt.20) | copy-start | bytes 4732
  37.3 64.2 %copy-start.4 = (f32[394,768]{1,0:T(8,128)}, f32[394,768]{1,0:T(8,128)S(1)}, u32[]{:S(2)}) copy-start(f32[394,768]{1,0:T(8,128)S(1)} %reshape.241) | copy-start | bytes 3631108
  37.5 66.9 %copy-start.36 = (s32[394,1]{0,1:T(1,128)}, s32[394,1]{0,1:T(1,128)S(1)}, u32[]{:S(2)}) copy-start(s32[394,1]{0,1:T(1,128)S(1)} %get-tuple-element.143) | copy-start | bytes 4732
  37.6 79.7 %copy-start.34 = (s32[394,1]{0,1:T(1,128)}, s32[394,1]{0,1:T(1,128)S(1)}, u32[]{:S(2)}) copy-start(s32[394,1]{0,1:T(1,128)S(1)} %get-tuple-element.142) | copy-start | bytes 4732
  76.4 0.6 copy-start.22
  76.4 0.6 copy-start.29
  90.3 7.5 %copy-start.8 = (bf16[2,197,12,64]{1,3,2,0:T(8,128)(2,1)}, bf16[2,197,12,64]{1,3,2,0:T(8,128)(2,1)S(1)}, u32[]{:S(2)}) copy-start(bf16[2,197,12,64]{1,3,2,0:T(8,128)(2,1)S(1)} %copy.172) | copy-start | bytes 1815556
  94.6 3.3 copy-start.6
  96.9 2.3 copy-start
  101.5 2.7 copy-start.17
  104.4 16.4 %copy-start.12 = (bf16[394,768]{1,0:T(8,128)(2,1)}, bf16[394,768]{1,0:T(8,128)(2,1)S(1)}, u32[]{:S(2)}) copy-start(bf16[394,768]{1,0:T(8,128)(2,1)S(1)} %add_convert_fusion.1) | copy-start | bytes 1815556
  106.9 4.7 copy-start.24
  106.9 9.8 %copy-start.33 = (bf16[1,768]{1,0:T(2,128)(2,1)S(1)}, bf16[1,768]{1,0:T(2,128)(2,1)}, u32[]{:S(2)}) copy-start(bf16[1,768]{1,0:T(2,128)(2,1)} %param.33) | copy-start | bytes 4612
  106.9 10.5 %copy-start.37 = (s32[394,1]{0,1:T(1,128)S(1)}, s32[394,1]{0,1:T(1,128)}, u32[]{:S(2)}) copy-start(s32[394,1]{0,1:T(1,128)} %copy-done.36) | copy-start | bytes 4732
  106.9 43.2 %all-to-all-start = ((bf16[4,264,768]{2,1,0:T(8,128)(2,1)}), bf16[4,264,768]{2,1,0:T(8,128)(2,1)S(1)}, u32[]{:S(2)}, u32[]{:S(2)}) async-start(bf16[4,264,768]{2,1,0:T(8,128)(2,1)} %bitcast.137), calls=%async_computation | async-start | bytes 3244032 | tf_op jit(solution)/shard_map/all_to_all | solution.py:94
  150.0 1.2 copy-start.10
  150.0 7.3 %copy-start.40 = (pred[4]{0:T(512)(128)(4,1)S(1)}, pred[4]{0:T(512)(128)(4,1)}, u32[]{:S(2)}) copy-start(pred[4]{0:T(512)(128)(4,1)} %iota_compare_fusion.9) | copy-start | bytes 16
  151.2 41.6 %all-to-all-start.2 = ((bf16[4,264,768]{2,1,0:T(8,128)(2,1)}), bf16[4,264,768]{2,1,0:T(8,128)(2,1)S(1)}, u32[]{:S(2)}, u32[]{:S(2)}) async-start(bf16[4,264,768]{2,1,0:T(8,128)(2,1)} %bitcast.135), calls=%async_computation.2 | async-start | bytes 3244032 | tf_op jit(solution)/shard_map/all_to_all | solution.py:94
  157.5 12.2 %copy-start.31 = (f32[768]{0:T(1024)S(1)}, f32[768]{0:T(1024)}, u32[]{:S(2)}) copy-start(f32[768]{0:T(1024)} %convert_reduce_fusion.4) | copy-start | bytes 9220
  165.1 4.6 copy-start.42
  192.8 44.7 %all-to-all-start.1 = ((bf16[4,264,768]{2,1,0:T(8,128)(2,1)}), bf16[4,264,768]{2,1,0:T(8,128)(2,1)}, u32[]{:S(2)}, u32[]{:S(2)}) async-start(bf16[4,264,768]{2,1,0:T(8,128)(2,1)} %bitcast.136), calls=%async_computation.1 | async-start | bytes 3244032 | tf_op jit(solution)/shard_map/all_to_all | solution.py:94
  213.6 15.0 %copy-start.41 = (bf16[1056,3072]{1,0:T(8,128)(2,1)}, bf16[1056,3072]{1,0:T(8,128)(2,1)S(1)}, u32[]{:S(2)}) copy-start(bf16[1056,3072]{1,0:T(8,128)(2,1)S(1)} %get-tuple-element.158) | copy-start | bytes 19464196
  237.5 5.2 copy-start.11
  237.5 42.3 %all-to-all-start.3 = ((bf16[4,264,768]{2,1,0:T(8,128)(2,1)}), bf16[4,264,768]{2,1,0:T(8,128)(2,1)}, u32[]{:S(2)}, u32[]{:S(2)}) async-start(bf16[4,264,768]{2,1,0:T(8,128)(2,1)} %bitcast.134), calls=%async_computation.3 | async-start | bytes 3244032 | tf_op jit(solution)/shard_map/all_to_all | solution.py:94
  242.7 149.9 %all-reduce.8.cloned.1.call-start = ((), (), s32[]{:S(2)}) async-start(), calls=%async_computation.8 | async-start | bytes 18874368 | tf_op jit(solution)/shard_map/psum | solution.py:203
  253.7 0.7 copy-start.39
  253.7 0.7 copy-start.38
  253.7 230.5 %reduce-scatter.2.cloned.1.call-start = ((), (), s32[]{:S(2)}) async-start(), calls=%async_computation.5 | async-start | bytes 6144000 | tf_op jit(solution)/shard_map/reduce_scatter | solution.py:292
  254.4 2.5 copy-start.20
  254.4 2.5 copy-start.35
  279.8 2.7 copy-start.21
  285.9 1.0 copy-start.2
  296.9 2.2 copy-start.7
  297.7 5.4 slice-start
  299.1 4.1 slice-start.1
  303.2 1.2 copy-start.9
  312.2 2.1 copy-start.19
  313.0 2.7 copy-start.18
  314.3 1.5 copy-start.5
  314.3 1.5 copy-start.23
  314.3 1.5 copy-start.26
  314.3 1.5 copy-start.28
  315.9 6.2 %copy-start.15 = (bf16[394,2304]{0,1:T(8,128)(2,1)}, bf16[394,2304]{0,1:T(8,128)(2,1)S(1)}, u32[]{:S(2)}) copy-start(bf16[394,2304]{0,1:T(8,128)(2,1)S(1)} %constant_dynamic-update-slice_fusion) | copy-start | bytes 5446660
  322.0 2.4 copy-start.13
  322.0 3.1 copy-start.3
  324.4 2.9 copy-start.30
  325.2 2.1 copy-start.16
  332.2 213.0 %all-reduce.6.cloned.1.call-start = ((), (), s32[]{:S(2)}) async-start(), calls=%async_computation.6 | async-start | bytes 2457600 | tf_op jit(solution)/shard_map/psum | solution.py:296
  484.2 7.6 %slice-start.2 = ((s8[4718592]{0:T(1024)(128)(4,1)}), s8[524288]{0:T(1024)(128)(4,1)S(1)}, s32[]{:S(2)}) async-start(s8[4718592]{0:T(1024)(128)(4,1)} %bitcast.123), calls=%async_computation.11 | async-start | bytes 1048576
  484.2 7.5 %slice-start.3 = ((s8[4718592]{0:T(1024)(128)(4,1)}), s8[4194304]{0:T(1024)(128)(4,1)S(1)}, s32[]{:S(2)}) async-start(s8[4718592]{0:T(1024)(128)(4,1)} %bitcast.123), calls=%async_computation.12 | async-start | bytes 8388608
  545.2 4.1 copy-start.1
Sparse Core Ops, SparseCore 0:
  32.6 41.3 all-gather.3
  253.8 138.7 all-reduce.7
  395.6 88.5 reduce-scatter.1
  487.2 57.9 all-reduce.5
